TPU v7x, 32 devices: a whole 2x2x4 slice. The times are simulated.
32 devices in a mesh: groups: 2 (over y), dom: 4 (over x, core), sub: 4 (over z).
Axes of the slice: x: 2, y: 2, z: 4, core: 2. Of those that a mesh axis runs over, the one named last changes fastest.
Arguments:
- node_states: float32 [8192, 512], P(('groups', 'dom', 'sub')), parts along dimension 0, may hold values from -6 to 6
- node_pre: float32 [8192, 512], P(('groups', 'dom', 'sub')), parts along dimension 0, may hold values from -6 to 6
- edge_states: float32 [4096, 512], P(('groups', 'dom', 'sub')), parts along dimension 0, may hold values from -6 to 6
- edge_pre: float32 [4096, 512], P(('groups', 'dom', 'sub')), parts along dimension 0, may hold values from -6 to 6
- node_cotangent: float32 [8192, 512], P(('groups', 'dom', 'sub')), parts along dimension 0, may hold values from -6 to 6
- edge_cotangent: float32 [4096, 512], P(('groups', 'dom', 'sub')), parts along dimension 0, may hold values from -6 to 6
- endpoints: int32 [2, 4096], P(None, ('groups', 'dom', 'sub')), parts along dimension 1, may hold values from 0 to 319, as said below
- send_lists: int32 [32, 4, 16], P(('groups', 'dom', 'sub')), parts along dimension 0, may hold values from 0 to 255, as said below
- node_counts: int32 [32], P(('groups', 'dom', 'sub')), parts along dimension 0, may hold values from 128 to 256
- edge_blocks: int32 [32], P(('groups', 'dom', 'sub')), parts along dimension 0, may hold values from 1 to 1
- edge_first: float32 [1536, 512], P(('dom', 'sub')), may hold values from -0.15625 to 0.15625
- edge_second: float32 [512, 512], P(('dom', 'sub')), may hold values from -0.25 to 0.25
- edge_bias: float32 [512], P(('dom', 'sub')), may hold values from -3 to 3
- edge_gain: float32 [512], P(('dom', 'sub')), may hold values from 0.5 to 1.5
- edge_shift: float32 [512], P(('dom', 'sub')), may hold values from -3 to 3
- node_first: float32 [1024, 512], P(('dom', 'sub')), may hold values from -0.1875 to 0.1875
- node_second: float32 [512, 512], P(('dom', 'sub')), may hold values from -0.25 to 0.25
- node_bias: float32 [512], P(('dom', 'sub')), may hold values from -3 to 3
- node_gain: float32 [512], P(('dom', 'sub')), may hold values from 0.5 to 1.5
Outputs:
- edge_grads: float32 [4096, 512], P(('groups', 'dom', 'sub')), parts along dimension 0
- node_grads: float32 [8192, 512], P(('groups', 'dom', 'sub')), parts along dimension 0
- edge_first_grad: float32 [3072, 512], P(('groups', 'dom', 'sub')), parts along dimension 0
- edge_second_grad: float32 [1024, 512], P(('groups', 'dom', 'sub')), parts along dimension 0
- node_first_grad: float32 [2048, 512], P(('groups', 'dom', 'sub')), parts along dimension 0
- node_second_grad: float32 [1024, 512], P(('groups', 'dom', 'sub')), parts along dimension 0
There are 2 independent parts, one for each index of `groups`. A program takes and returns all parts, laid end to end along the dimension named above; an argument that names none is the same for every part. Nothing has to cross between parts.
Inputs may be any that keep to these rules, and one draw needn't show every extreme that they name: `endpoints`: sender slots are a live local node below node_counts of the device, or a ghost slot 256 + k * 16 + j whose neighbour k exists; receiver slots are live local nodes. `send_lists`: every entry is a live node of its device.
All inputs are finite; a program needn't handle non-finite values.
Results may differ from a plain program's by a relative error of at most 0.0003.
Values sent between devices are 32-bit elements; how exact they have to be, the bound alone decides.
A program may use at most 128 MiB of HBM per device.

v0:
```python
import math

import jax
import jax.numpy as jnp
from jax import lax
from jax.sharding import PartitionSpec as P

EPSILON = 1e-05


def padded(cells, sides, width):
    for axis, dim in sides:
        count = lax.axis_size(axis)
        ends = count - 1
        head = lax.slice_in_dim(cells, 0, width, axis=dim)
        tail = lax.slice_in_dim(cells, cells.shape[dim] - width, cells.shape[dim], axis=dim)
        cells = jnp.concatenate(
            [
                lax.ppermute(tail, axis, [(i, (i + 1) % count) for i in range(ends)]),
                cells,
                lax.ppermute(head, axis, [((i + 1) % count, i) for i in range(ends)]),
            ],
            axis=dim,
        )
    return cells


def matmul(left, right):
    return jnp.dot(left, right, precision=lax.Precision.HIGHEST, preferred_element_type=jnp.float32)


def inner(left, right):
    return lax.dot_general(
        left,
        right,
        (((0,), (0,)), ((), ())),
        precision=lax.Precision.HIGHEST,
        preferred_element_type=jnp.float32,
    )


def outer_back(left, right):
    return lax.dot_general(
        left,
        right,
        (((1,), (1,)), ((), ())),
        precision=lax.Precision.HIGHEST,
        preferred_element_type=jnp.float32,
    )


def layer_norm(values):
    center = values - jnp.mean(values, axis=-1, keepdims=True)
    inverse = 1.0 / jnp.sqrt(jnp.mean(center * center, axis=-1, keepdims=True) + EPSILON)
    return (center * inverse, inverse)


def norm_back(upstream, normed, inverse):
    first = jnp.mean(upstream, axis=-1, keepdims=True)
    second = jnp.mean(upstream * normed, axis=-1, keepdims=True)
    return inverse * (upstream - first - normed * second)


def shards(
    node_states,
    node_pre,
    edge_states,
    edge_pre,
    node_cotangent,
    edge_cotangent,
    endpoints,
    send_lists,
    node_counts,
    edge_blocks,
    edge_first,
    edge_second,
    edge_bias,
    edge_gain,
    edge_shift,
    node_first,
    node_second,
    node_bias,
    node_gain,
):
    node_rows, width = node_states.shape
    edge_rows = edge_states.shape[0]
    ghost = send_lists.shape[2]
    dom_count = lax.axis_size("dom")
    sub_count = lax.axis_size("sub")
    peer_count = dom_count * sub_count
    lists = send_lists[0]
    outgoing = jnp.take(node_states, lists.reshape(-1), axis=0).reshape(4, ghost, width)
    dom_side = padded(jnp.stack([outgoing[1], outgoing[0]]), (("dom", 0),), 1)
    sub_side = padded(jnp.stack([outgoing[3], outgoing[2]]), (("sub", 0),), 1)
    ghosts = jnp.stack([dom_side[0], dom_side[3], sub_side[0], sub_side[3]])
    ghosts = ghosts.reshape(4 * ghost, width)
    full_node_first, full_node_second, full_node_bias, full_node_gain = (
        lax.all_gather(node_first, ("dom", "sub"), axis=0, tiled=True),
        lax.all_gather(node_second, ("dom", "sub"), axis=0, tiled=True),
        lax.all_gather(node_bias, ("dom", "sub"), axis=0, tiled=True),
        lax.all_gather(node_gain, ("dom", "sub"), axis=0, tiled=True),
    )
    full_edge_first, full_edge_second, full_edge_bias, full_edge_gain, full_edge_shift = (
        lax.all_gather(edge_first, ("dom", "sub"), axis=0, tiled=True),
        lax.all_gather(edge_second, ("dom", "sub"), axis=0, tiled=True),
        lax.all_gather(edge_bias, ("dom", "sub"), axis=0, tiled=True),
        lax.all_gather(edge_gain, ("dom", "sub"), axis=0, tiled=True),
        lax.all_gather(edge_shift, ("dom", "sub"), axis=0, tiled=True),
    )
    live_nodes = (jnp.arange(node_rows) < node_counts[0]).astype(jnp.float32)[:, None]
    live_edges = (jnp.arange(edge_rows) < edge_blocks[0] * 128).astype(jnp.float32)[:, None]
    source = endpoints[0]
    target = endpoints[1]
    edge_scale = 1.0 / math.sqrt(edge_rows * peer_count)
    node_scale = 1.0 / math.sqrt(node_rows * peer_count)
    edge_act = jnp.maximum(edge_pre, 0.0)
    edge_normed, edge_inverse = layer_norm(matmul(edge_act, full_edge_second) + full_edge_bias)
    message = (edge_normed * full_edge_gain + full_edge_shift) * live_edges
    aggregate = jax.ops.segment_sum(message, target, node_rows)
    node_act = jnp.maximum(node_pre, 0.0)
    node_normed, node_inverse = layer_norm(matmul(node_act, full_node_second) + full_node_bias)
    node_upstream = node_cotangent * live_nodes
    node_grad_z = norm_back(node_upstream * full_node_gain, node_normed, node_inverse)
    node_grad_pre = outer_back(node_grad_z, full_node_second) * (node_pre > 0).astype(jnp.float32)
    node_input = jnp.concatenate([node_states, aggregate], axis=1)
    node_first_grad, node_second_grad = (
        lax.psum_scatter(
            inner(node_input, node_grad_pre) * node_scale,
            ("dom", "sub"),
            scatter_dimension=0,
            tiled=True,
        ),
        lax.psum_scatter(
            inner(node_act, node_grad_z) * node_scale,
            ("dom", "sub"),
            scatter_dimension=0,
            tiled=True,
        ),
    )
    node_grad_input = outer_back(node_grad_pre, full_node_first)
    state_grads = node_upstream + node_grad_input[:, :width]
    edge_upstream = (
        edge_cotangent + jnp.take(node_grad_input[:, width:], target, axis=0)
    ) * live_edges
    edge_grad_z = norm_back(edge_upstream * full_edge_gain, edge_normed, edge_inverse)
    edge_grad_pre = outer_back(edge_grad_z, full_edge_second) * (edge_pre > 0).astype(jnp.float32)
    edge_second_grad = lax.psum_scatter(
        inner(edge_act, edge_grad_z) * edge_scale, ("dom", "sub"), scatter_dimension=0, tiled=True
    )
    extended = jnp.concatenate([node_states, ghosts], axis=0)
    features = jnp.concatenate(
        [edge_states, jnp.take(extended, source, axis=0), jnp.take(extended, target, axis=0)],
        axis=1,
    )
    edge_first_grad = lax.psum_scatter(
        inner(features, edge_grad_pre) * edge_scale, ("dom", "sub"), scatter_dimension=0, tiled=True
    )
    edge_grad_input = outer_back(edge_grad_pre, full_edge_first)
    edge_grads = (edge_cotangent + edge_grad_input[:, :width]) * live_edges
    extended_grads = jax.ops.segment_sum(
        edge_grad_input[:, width : 2 * width], source, node_rows + 4 * ghost
    )
    extended_grads = extended_grads + jax.ops.segment_sum(
        edge_grad_input[:, 2 * width :], target, node_rows + 4 * ghost
    )
    state_grads = state_grads + extended_grads[:node_rows]
    ghost_grads = extended_grads[node_rows:].reshape(4, ghost, width)
    dom_back = padded(jnp.stack([ghost_grads[0], ghost_grads[1]]), (("dom", 0),), 1)
    sub_back = padded(jnp.stack([ghost_grads[2], ghost_grads[3]]), (("sub", 0),), 1)
    returned = jnp.stack([dom_back[3], dom_back[0], sub_back[3], sub_back[0]])
    state_grads = state_grads + jax.ops.segment_sum(
        returned.reshape(-1, width), lists.reshape(-1), node_rows
    )
    return (
        edge_grads,
        state_grads,
        edge_first_grad,
        edge_second_grad,
        node_first_grad,
        node_second_grad,
    )


def solution(mesh):
    in_specs = (
        P(("groups", "dom", "sub"), None),
        P(("groups", "dom", "sub"), None),
        P(("groups", "dom", "sub"), None),
        P(("groups", "dom", "sub"), None),
        P(("groups", "dom", "sub"), None),
        P(("groups", "dom", "sub"), None),
        P(None, ("groups", "dom", "sub")),
        P(("groups", "dom", "sub"), None, None),
        P(("groups", "dom", "sub")),
        P(("groups", "dom", "sub")),
        P(("dom", "sub"), None),
        P(("dom", "sub"), None),
        P(("dom", "sub")),
        P(("dom", "sub")),
        P(("dom", "sub")),
        P(("dom", "sub"), None),
        P(("dom", "sub"), None),
        P(("dom", "sub")),
        P(("dom", "sub")),
    )
    out_specs = (
        P(("groups", "dom", "sub"), None),
        P(("groups", "dom", "sub"), None),
        P(("groups", "dom", "sub"), None),
        P(("groups", "dom", "sub"), None),
        P(("groups", "dom", "sub"), None),
        P(("groups", "dom", "sub"), None),
    )
    return jax.shard_map(shards, mesh=mesh, in_specs=in_specs, out_specs=out_specs, check_vma=False)
```

profile of v0, /device:TPU:0, one launch (start us, length us, event | category | flops | bytes accessed | tf_op | source)
XLA Modules:
  0.0 442.2 jit_solution(13776215325105201834)
XLA Ops:
  7.2 0.7 all-gather.7.cloned.1.call-update
  8.0 0.7 all-gather.5.cloned.1.call-update
  8.7 0.7 all-gather.9.cloned.1.call-update
  10.7 1.2 dynamic-slice
  12.6 0.9 dynamic-update-slice
  13.4 0.8 dynamic-update-slice.1
  14.3 0.8 dynamic-update-slice.2
  15.1 0.8 dynamic-update-slice.3
  16.0 0.8 dynamic-update-slice.4
  16.8 63.6 %all-reduce.5 = (f32[512]{0:T(512)S(1)}, f32[512]{0:T(512)S(1)}, f32[512]{0:T(512)S(1)}, f32[512]{0:T(512)S(1)}, f32[512]{0:T(512)S(1)}) all-reduce(f32[512]{0:T(512)S(1)} %dynamic-update-slice.1, f32[512]{0:T(512)S(1)} %dynamic-update-slice.2, f32[512]{0:T(512)S(1)} %dynamic-update-slice.3, ...), channel_id=1, replica_groups=mesh['groups'=2,'dom'=4,'sub'=4] {'dom','sub'}, use_global_device_ids=true, to_apply=%add.1 | all-reduce | flops 2560 | bytes 20480
  80.4 2.5 fusion.44
  83.5 2.4 convolution_multiply_fusion.2
  86.7 3.5 all-gather.5.cloned.1.call-done
  90.2 2.0 fusion.43
  92.5 2.2 scatter_custom_fusion.2
  94.7 2.5 convolution_select_fusion
  97.3 3.2 convolution_multiply_fusion.1
  100.9 0.7 gather_fusion.1
  101.6 31.2 %all-gather.9.cloned.1.call-done = f32[1024,512]{1,0:T(8,128)} async-done(((f32[64,512]{1,0:T(8,128)}), f32[1024,512]{1,0:T(8,128)}) %all-gather.9.cloned.1.call-update) | async-done | bytes 2097168 | tf_op jit(solution)/shard_map/all_gather | solution.py:98
  132.8 3.5 fusion.45
  136.3 1.0 copy-done.5
  137.4 0.8 gather_fusion
  138.4 2.1 convolution_multiply_fusion.3
  140.6 2.2 collective-permute-start.4
  142.8 1.3 collective-permute-start.5
  144.1 2.4 collective-permute-start.6
  146.6 1.3 collective-permute-start.7
  147.9 0.7 collective-permute-done.6
  148.6 4.4 collective-permute-done.7
  153.0 0.8 gather_fusion.2
  153.8 1.5 gather_fusion.3
  155.2 1.1 broadcast_select_fusion
  156.3 1.2 convolution_select_fusion.1
  157.5 4.4 convolution_multiply_fusion
  162.0 17.1 %all-gather.11.cloned.1.call-done = f32[1536,512]{1,0:T(8,128)} async-done(((f32[96,512]{1,0:T(8,128)}), f32[1536,512]{1,0:T(8,128)}) %all-gather.11.cloned.1.call-update) | async-done | bytes 3145744 | tf_op jit(solution)/shard_map/all_gather | solution.py:104
  179.1 5.2 %fusion.46 = f32[128,1536]{1,0:T(8,128)S(1)} fusion(f32[128,512]{1,0:T(8,128)S(1)} %convolution_select_fusion.1, f32[1536,512]{1,0:T(8,128)} %all-gather.11.cloned.1.call-done), kind=kOutput, calls=%fused_computation.115 | convolution fusion | flops 1207959552 | bytes 4194304 | tf_op jit(solution)/shard_map/dot_general | solution.py:43
  184.3 0.8 fusion.42
  185.1 2.3 scatter_custom_fusion
  187.4 1.3 collective-permute-start
  188.7 3.0 collective-permute-start.1
  191.8 1.3 collective-permute-start.2
  193.1 4.5 %collective-permute-start.3 = (f32[1,16,512]{2,1,0:T(8,128)S(1)}, f32[1,16,512]{2,1,0:T(8,128)S(1)}, u32[]{:S(2)}, u32[]{:S(2)}) collective-permute-start(f32[1,16,512]{2,1,0:T(8,128)S(1)} %get-tuple-element.25), channel_id=1, source_target_pairs={{0,1},{1,2},{2,3},{4,5},{5,6},{6,7},{8,9},{9,10},{10,11},{12,13},{... | collective-permute-start | bytes 98312 | tf_op jit(solution)/shard_map/ppermute | solution.py:19
  197.8 1.4 collective-permute-done.3
  199.2 1.2 scatter_fusion
  200.4 38.9 %reduce-scatter.11.cloned.1.call-done = f32[32,512]{1,0:T(8,128)} async-done(((f32[512,512]{1,0:T(8,128)}), f32[32,512]{1,0:T(8,128)}) %reduce-scatter.11.cloned.1.call-update) | async-done | bytes 65552 | tf_op jit(solution)/shard_map/reduce_scatter | solution.py:133
  239.4 65.3 %reduce-scatter.9.cloned.1.call-done = f32[64,512]{1,0:T(8,128)} async-done(((f32[1024,512]{1,0:T(8,128)}), f32[64,512]{1,0:T(8,128)}) %reduce-scatter.9.cloned.1.call-update) | async-done | bytes 131088 | tf_op jit(solution)/shard_map/reduce_scatter | solution.py:127
  304.7 60.6 %reduce-scatter.7.cloned.1.call-done = f32[32,512]{1,0:T(8,128)} async-done(((f32[512,512]{1,0:T(8,128)}), f32[32,512]{1,0:T(8,128)}) %reduce-scatter.7.cloned.1.call-update) | async-done | bytes 65552 | tf_op jit(solution)/shard_map/reduce_scatter | solution.py:147
  365.3 70.1 %reduce-scatter.5.cloned.1.call-done = f32[96,512]{1,0:T(8,128)} async-done(((f32[1536,512]{1,0:T(8,128)}), f32[96,512]{1,0:T(8,128)}) %reduce-scatter.5.cloned.1.call-update) | async-done | bytes 196624 | tf_op jit(solution)/shard_map/reduce_scatter | solution.py:155
  (84 shorter events, 2.7 us)
Async XLA Ops:
  7.2 76.3 %copy-start.2 = (f32[256,512]{1,0:T(8,128)S(1)}, f32[256,512]{1,0:T(8,128)}, u32[]{:S(2)}) copy-start(f32[256,512]{1,0:T(8,128)} %param.22) | copy-start | bytes 1572868
  7.2 76.0 %copy-start.1 = (f32[256,512]{1,0:T(8,128)S(1)}, f32[256,512]{1,0:T(8,128)}, u32[]{:S(2)}) copy-start(f32[256,512]{1,0:T(8,128)} %param.25) | copy-start | bytes 1572868
  7.2 73.2 %all-gather.7.cloned.1.call-start = ((), (), s32[]{:S(2)}) async-start(), calls=%async_computation.5 | async-start | bytes 1114112 | tf_op jit(solution)/shard_map/all_gather | solution.py:99
  7.9 82.3 %all-gather.5.cloned.1.call-start = ((), (), s32[]{:S(2)}) async-start(), calls=%async_computation.4 | async-start | bytes 1114112 | tf_op jit(solution)/shard_map/all_gather | solution.py:105
  8.7 124.1 %all-gather.9.cloned.1.call-start = ((), (), s32[]{:S(2)}) async-start(), calls=%async_computation.6 | async-start | bytes 2228224 | tf_op jit(solution)/shard_map/all_gather | solution.py:98
  9.4 169.7 %all-gather.11.cloned.1.call-start = ((), (), s32[]{:S(2)}) async-start(), calls=%async_computation.7 | async-start | bytes 3342336 | tf_op jit(solution)/shard_map/all_gather | solution.py:104
  10.0 229.4 %reduce-scatter.11.cloned.1.call-start = ((), (), s32[]{:S(2)}) async-start(), calls=%async_computation.11 | async-start | bytes 1114112 | tf_op jit(solution)/shard_map/reduce_scatter | solution.py:133
  82.9 3.0 copy-start.13
  83.0 7.3 %copy-start.7 = (f32[128,512]{1,0:T(8,128)S(1)}, f32[128,512]{1,0:T(8,128)}, u32[]{:S(2)}) copy-start(f32[128,512]{1,0:T(8,128)} %param.24) | copy-start | bytes 786436
  85.9 11.3 %copy-start = (f32[256,512]{1,0:T(8,128)S(1)}, f32[256,512]{1,0:T(8,128)}, u32[]{:S(2)}) copy-start(f32[256,512]{1,0:T(8,128)} %param.21) | copy-start | bytes 1572868
  85.9 218.7 %reduce-scatter.9.cloned.1.call-start = ((), (), s32[]{:S(2)}) async-start(), calls=%async_computation.10 | async-start | bytes 2228224 | tf_op jit(solution)/shard_map/reduce_scatter | solution.py:127
  94.7 2.5 copy-start.8
  97.2 3.5 copy-start.12
  100.5 264.8 %reduce-scatter.7.cloned.1.call-start = ((), (), s32[]{:S(2)}) async-start(), calls=%async_computation.9 | async-start | bytes 1114112 | tf_op jit(solution)/shard_map/reduce_scatter | solution.py:147
  101.6 36.5 %copy-start.9 = (f32[128,512]{1,0:T(8,128)S(1)}, f32[128,512]{1,0:T(8,128)}, u32[]{:S(2)}) copy-start(f32[128,512]{1,0:T(8,128)} %param.26) | copy-start | bytes 786436
  136.3 1.0 copy-start.5
  140.5 294.9 %reduce-scatter.5.cloned.1.call-start = ((), (), s32[]{:S(2)}) async-start(), calls=%async_computation.8 | async-start | bytes 3342336 | tf_op jit(solution)/shard_map/reduce_scatter | solution.py:155
  140.6 7.2 %collective-permute-start.4 = (f32[1,16,512]{2,1,0:T(8,128)S(1)}, f32[1,16,512]{2,1,0:T(8,128)S(1)}, u32[]{:S(2)}, u32[]{:S(2)}) collective-permute-start(f32[1,16,512]{2,1,0:T(8,128)S(1)} %get-tuple-element.28), channel_id=1, source_target_pairs={{0,4},{4,8},{8,12},{1,5},{5,9},{9,13},{2,6},{6,10},{10,14},{3,7},{... | collective-permute-start | bytes 98312 | tf_op jit(solution)/shard_map/ppermute | solution.py:19
  142.8 5.1 %collective-permute-start.5 = (f32[1,16,512]{2,1,0:T(8,128)S(1)}, f32[1,16,512]{2,1,0:T(8,128)S(1)}, u32[]{:S(2)}, u32[]{:S(2)}) collective-permute-start(f32[1,16,512]{2,1,0:T(8,128)S(1)} %get-tuple-element.31), channel_id=1, source_target_pairs={{4,0},{8,4},{12,8},{5,1},{9,5},{13,9},{6,2},{10,6},{14,10},{7,3},{... | collective-permute-start | bytes 98312 | tf_op jit(solution)/shard_map/ppermute | solution.py:21
  144.1 4.4 %collective-permute-start.6 = (f32[1,16,512]{2,1,0:T(8,128)S(1)}, f32[1,16,512]{2,1,0:T(8,128)S(1)}, u32[]{:S(2)}, u32[]{:S(2)}) collective-permute-start(f32[1,16,512]{2,1,0:T(8,128)S(1)} %get-tuple-element.30), channel_id=1, source_target_pairs={{0,1},{1,2},{2,3},{4,5},{5,6},{6,7},{8,9},{9,10},{10,11},{12,13},{... | collective-permute-start | bytes 98312 | tf_op jit(solution)/shard_map/ppermute | solution.py:19
  146.6 6.4 %collective-permute-start.7 = (f32[1,16,512]{2,1,0:T(8,128)S(1)}, f32[1,16,512]{2,1,0:T(8,128)S(1)}, u32[]{:S(2)}, u32[]{:S(2)}) collective-permute-start(f32[1,16,512]{2,1,0:T(8,128)S(1)} %get-tuple-element.29), channel_id=1, source_target_pairs={{1,0},{2,1},{3,2},{5,4},{6,5},{7,6},{9,8},{10,9},{11,10},{13,12},{... | collective-permute-start | bytes 98312 | tf_op jit(solution)/shard_map/ppermute | solution.py:21
  153.0 3.3 copy-start.4
  155.2 2.3 copy-start.11
  161.9 22.4 %copy-start.10 = (f32[128,512]{1,0:T(8,128)S(1)}, f32[128,512]{1,0:T(8,128)}, u32[]{:S(2)}) copy-start(f32[128,512]{1,0:T(8,128)} %param.26) | copy-start | bytes 786436
  162.0 35.7 %copy-start.6 = (f32[256,1024]{1,0:T(8,128)S(1)}, f32[256,1024]{1,0:T(8,128)}, u32[]{:S(2)}) copy-start(f32[256,1024]{1,0:T(8,128)} %copy-done.5) | copy-start | bytes 3145732
  187.4 10.3 %collective-permute-start = (f32[1,16,512]{2,1,0:T(8,128)S(1)}, f32[1,16,512]{2,1,0:T(8,128)S(1)}, u32[]{:S(2)}, u32[]{:S(2)}) collective-permute-start(f32[1,16,512]{2,1,0:T(8,128)S(1)} %get-tuple-element.24), channel_id=1, source_target_pairs={{4,0},{8,4},{12,8},{5,1},{9,5},{13,9},{6,2},{10,6},{14,10},{7,3},{... | collective-permute-start | bytes 98312 | tf_op jit(solution)/shard_map/ppermute | solution.py:21
  188.7 9.1 %collective-permute-start.1 = (f32[1,16,512]{2,1,0:T(8,128)S(1)}, f32[1,16,512]{2,1,0:T(8,128)S(1)}, u32[]{:S(2)}, u32[]{:S(2)}) collective-permute-start(f32[1,16,512]{2,1,0:T(8,128)S(1)} %get-tuple-element.27), channel_id=1, source_target_pairs={{0,4},{4,8},{8,12},{1,5},{5,9},{9,13},{2,6},{6,10},{10,14},{3,7},{... | collective-permute-start | bytes 98312 | tf_op jit(solution)/shard_map/ppermute | solution.py:19
  191.8 6.0 %collective-permute-start.2 = (f32[1,16,512]{2,1,0:T(8,128)S(1)}, f32[1,16,512]{2,1,0:T(8,128)S(1)}, u32[]{:S(2)}, u32[]{:S(2)}) collective-permute-start(f32[1,16,512]{2,1,0:T(8,128)S(1)} %get-tuple-element.26), channel_id=1, source_target_pairs={{1,0},{2,1},{3,2},{5,4},{6,5},{7,6},{9,8},{10,9},{11,10},{13,12},{... | collective-permute-start | bytes 98312 | tf_op jit(solution)/shard_map/ppermute | solution.py:21
  193.1 6.1 %collective-permute-start.3 = (f32[1,16,512]{2,1,0:T(8,128)S(1)}, f32[1,16,512]{2,1,0:T(8,128)S(1)}, u32[]{:S(2)}, u32[]{:S(2)}) collective-permute-start(f32[1,16,512]{2,1,0:T(8,128)S(1)} %get-tuple-element.25), channel_id=1, source_target_pairs={{0,1},{1,2},{2,3},{4,5},{5,6},{6,7},{8,9},{9,10},{10,11},{12,13},{... | collective-permute-start | bytes 98312 | tf_op jit(solution)/shard_map/ppermute | solution.py:19
  200.4 235.0 %copy-start.3 = (f32[256,512]{1,0:T(8,128)}, f32[256,512]{1,0:T(8,128)S(1)}, u32[]{:S(2)}) copy-start(f32[256,512]{1,0:T(8,128)S(1)} %scatter_fusion) | copy-start | bytes 1572868
Sparse Core Ops, SparseCore 0:
  10.2 40.7 all-gather.6
  53.2 36.9 all-gather.4
  92.4 40.3 all-gather.8
  135.0 44.1 all-gather.10
  183.2 56.1 reduce-scatter.10
  244.0 60.6 reduce-scatter.8
  308.9 56.3 reduce-scatter.6
  370.2 65.1 reduce-scatter.4
where the time goes:
time: 443 us; the launch traced here: 442 us
  waiting for transfers between devices  296 us (67%)
  blocking collectives  63.6 us (14%)
  matrix products  29 us (7%)
  starting transfers between devices  17.8 us (4%)
  between operations  16.6 us (4%)
  local copies, waits for them, and re-layouts  10.4 us (2%)
  other arithmetic  8.89 us (2%)
    reduce_scatter x1, waiting for transfers between devices, shards(): lax.psum_scatter(inner(features, edge_grad_pre) * edge_scale, ('dom', 'su...  70.1 us
    reduce_scatter x1, waiting for transfers between devices, shards(): lax.psum_scatter(inner(node_input, node_grad_pre) * node_scale, ('dom', '...  65.3 us
    unnamed x1, blocking collectives  63.6 us
    reduce_scatter x1, waiting for transfers between devices, shards(): lax.psum_scatter(inner(edge_act, edge_grad_z) * edge_scale, ('dom', 'sub'...  60.6 us
    reduce_scatter x1, waiting for transfers between devices, shards(): lax.psum_scatter(inner(node_act, node_grad_z) * node_scale, ('dom', 'sub'...  38.9 us
    all_gather x1, waiting for transfers between devices, shards(): lax.all_gather(node_first, ('dom', 'sub'), axis=0, tiled=True)  31.2 us
    all_gather x1, waiting for transfers between devices, shards(): lax.all_gather(edge_first, ('dom', 'sub'), axis=0, tiled=True)  17.1 us
    dot_general x4, matrix products, outer_back(): lax.dot_general(left, right, (((1,), (1,)), ((), ())), precision=lax.Prec...  12.4 us
  transfers between devices with their start and end apart: 16, of which 10 were waited for; matrix products, arithmetic and copies ran while one was open for 11% of the time, Pallas kernels for 0%

commit v1 on v0

--- a/solution.py
+++ b/solution.py
@@ -1,8 +1,11 @@
+import functools
 import math
 
 import jax
 import jax.numpy as jnp
 from jax import lax
+from jax.experimental import pallas as pl
+from jax.experimental.pallas import tpu as pltpu
 from jax.sharding import PartitionSpec as P
 
 EPSILON = 1e-05
@@ -61,7 +64,7 @@
     return inverse * (upstream - first - normed * second)
 
 
-def shards(
+def plain_shards(
     node_states,
     node_pre,
     edge_states,
@@ -181,6 +184,516 @@
     )
 
 
+MESH = pl.DeviceIdType.MESH
+UNIT = 32
+
+
+def split(values):
+    high = values.astype(jnp.bfloat16)
+    return (high, (values - high.astype(jnp.float32)).astype(jnp.bfloat16))
+
+
+def product(left, right, dims):
+    return lax.dot_general(
+        left, right, ((dims[:1], dims[1:]), ((), ())), preferred_element_type=jnp.float32
+    )
+
+
+def wide(left, right, dims):
+    return (
+        product(left[0], right[1], dims)
+        + product(left[1], right[0], dims)
+        + product(left[0], right[0], dims)
+    )
+
+
+def picked(picks, right, dims=(1, 0)):
+    return product(picks, right[1], dims) + product(picks, right[0], dims)
+
+
+def picks_of(slots, rows, first=0):
+    place = lax.broadcasted_iota(jnp.int32, (rows, slots.shape[1]), 0) + first
+    ones = jnp.where(place == slots, 1.0, 0.0).astype(jnp.float32)
+    return (ones.astype(jnp.bfloat16), ones.T.astype(jnp.bfloat16))
+
+
+def layer_kernel(
+    edge_scale,
+    node_scale,
+    counts,
+    blocks,
+    endpoints,
+    lists,
+    node_states,
+    node_pre,
+    edge_states,
+    edge_pre,
+    node_cotangent,
+    edge_cotangent,
+    own_a,
+    own_b,
+    own_c,
+    own_d,
+    edge_grads,
+    node_grads,
+    edge_first_grad,
+    edge_second_grad,
+    node_first_grad,
+    node_second_grad,
+    all_a,
+    all_b,
+    all_c,
+    all_d,
+    sum_b,
+    sum_c,
+    sum_a,
+    sum_d,
+    from_core,
+    from_x,
+    from_sub,
+    outgoing,
+    ghosts,
+    ghost_grads,
+    returned,
+    gather_send,
+    gather_recv,
+    core_send,
+    core_recv,
+    x_send,
+    x_recv,
+    sub_send,
+    sub_recv,
+    halo_send,
+    halo_recv,
+):
+    doms = all_a.shape[0]
+    subs = all_a.shape[1]
+    width = node_states.shape[1]
+    node_rows = node_states.shape[0]
+    edge_rows = edge_states.shape[0]
+    ghost = outgoing.shape[1]
+    dom = lax.axis_index("dom")
+    sub = lax.axis_index("sub")
+    x_mate = lax.rem(dom + 2, doms)
+    core_mate = dom + 1 - 2 * lax.rem(dom, 2)
+    far_mate = x_mate + 1 - 2 * lax.rem(x_mate, 2)
+
+    def before(step):
+        return lax.rem(sub + subs - step, subs)
+
+    def after(step):
+        return lax.rem(sub + step, subs)
+
+    barrier = pltpu.get_barrier_semaphore()
+    for step in range(1, doms):
+        pl.semaphore_signal(
+            barrier, inc=1, device_id={"dom": lax.rem(dom + step, doms)}, device_id_type=MESH
+        )
+    for step in range(1, subs):
+        pl.semaphore_signal(barrier, inc=1, device_id={"sub": after(step)}, device_id_type=MESH)
+    pl.semaphore_wait(barrier, doms + subs - 2)
+
+    def remote(source, target, send, recv, device):
+        return pltpu.make_async_remote_copy(
+            src_ref=source,
+            dst_ref=target,
+            send_sem=send,
+            recv_sem=recv,
+            device_id=device,
+            device_id_type=MESH,
+        )
+
+    owns = (own_a, own_b, own_c, own_d)
+    alls = (all_a, all_b, all_c, all_d)
+    pending = []
+
+    def gather_copy(part, index, source, slot, device):
+        return remote(
+            source,
+            alls[part].at[slot[0], slot[1]],
+            gather_send.at[part, index],
+            gather_recv.at[part, index],
+            device,
+        )
+
+    def gather_start(part, index, source, slot, device):
+        copy = gather_copy(part, index, source, slot, device)
+        copy.start()
+        pending.append(copy)
+
+    def gather_wait(part, index, slot):
+        place = alls[part].at[slot[0], slot[1]]
+        gather_copy(part, index, place, slot, {"dom": core_mate}).wait_recv()
+
+    def to_x(part, step, source):
+        gather_start(part, subs - 1 + step, source, (dom, before(step)), {"dom": x_mate})
+
+    def to_core(part, step, source):
+        gather_start(part, 2 * subs - 1 + step, source, (dom, before(step)), {"dom": core_mate})
+
+    def gather_first(part):
+        for step in range(1, subs):
+            gather_start(part, step - 1, owns[part], (dom, sub), {"sub": after(step)})
+        to_x(part, 0, owns[part])
+        to_core(part, 0, owns[part])
+
+    def gather_from_sub(part):
+        for step in range(1, subs):
+            slot = (dom, before(step))
+            gather_wait(part, step - 1, slot)
+            to_x(part, step, alls[part].at[slot[0], slot[1]])
+            to_core(part, step, alls[part].at[slot[0], slot[1]])
+
+    def gather_from_x(part):
+        for step in range(subs):
+            slot = (x_mate, before(step))
+            gather_wait(part, subs - 1 + step, slot)
+            gather_start(
+                part,
+                3 * subs - 1 + step,
+                alls[part].at[slot[0], slot[1]],
+                slot,
+                {"dom": core_mate},
+            )
+
+    def gather_from_core(part):
+        for step in range(subs):
+            gather_wait(part, 2 * subs - 1 + step, (core_mate, before(step)))
+            gather_wait(part, 3 * subs - 1 + step, (far_mate, before(step)))
+
+    sums = (sum_b, sum_c, sum_a, sum_d)
+    results = (node_second_grad, node_first_grad, edge_second_grad, edge_first_grad)
+    units = [
+        (which, first)
+        for which in range(4)
+        for first in range(0, sums[which].shape[2], UNIT)
+    ]
+
+    def unit_rows(unit, which_dom):
+        which, first = units[unit]
+        return sums[which].at[which_dom, :, pl.ds(first, UNIT), :]
+
+    def core_copies(unit):
+        return [
+            remote(
+                unit_rows(unit, target),
+                from_core.at[unit, index],
+                core_send.at[unit, index],
+                core_recv.at[unit, index],
+                {"dom": core_mate},
+            )
+            for index, target in enumerate((far_mate, core_mate))
+        ]
+
+    def x_copy(unit):
+        return remote(
+            unit_rows(unit, x_mate),
+            from_x.at[unit],
+            x_send.at[unit],
+            x_recv.at[unit],
+            {"dom": x_mate},
+        )
+
+    def sub_copies(unit):
+        which, first = units[unit]
+        return [
+            remote(
+                sums[which].at[dom, after(step), pl.ds(first, UNIT), :],
+                from_sub.at[unit, step - 1],
+                sub_send.at[unit, step - 1],
+                sub_recv.at[unit, step - 1],
+                {"sub": after(step)},
+            )
+            for step in range(1, subs)
+        ]
+
+    def reduce_core(unit):
+        for copy in core_copies(unit):
+            copy.start()
+
+    def reduce_x(unit):
+        far, near = core_copies(unit)
+        far.wait_recv()
+        rows = unit_rows(unit, x_mate)
+        rows[...] = rows[...] + from_core[unit, 0]
+        x_copy(unit).start()
+        near.wait_recv()
+        rows = unit_rows(unit, dom)
+        rows[...] = rows[...] + from_core[unit, 1]
+
+    def reduce_sub(unit):
+        x_copy(unit).wait_recv()
+        rows = unit_rows(unit, dom)
+        rows[...] = rows[...] + from_x[unit]
+        for copy in sub_copies(unit):
+            copy.start()
+
+    def reduce_last(unit):
+        which, first = units[unit]
+        total = sums[which][dom, sub, pl.ds(first, UNIT), :]
+        for step, copy in enumerate(sub_copies(unit)):
+            copy.wait_recv()
+            total = total + from_sub[unit, step]
+        results[which][pl.ds(first, UNIT), :] = total
+
+    def halo_copies(source, target, turn):
+        ways = (
+            {"dom": lax.rem(dom + 1, doms)},
+            {"dom": lax.rem(dom + doms - 1, doms)},
+            {"sub": after(1)},
+            {"sub": before(1)},
+        )
+        return [
+            remote(
+                source.at[index],
+                target.at[index],
+                halo_send.at[turn, index],
+                halo_recv.at[turn, index],
+                ways[index + (1 - 2 * (index % 2)) * turn],
+            )
+            for index in range(4)
+        ]
+
+    for part in range(4):
+        gather_first(part)
+    for part in range(4):
+        alls[part][dom, sub] = owns[part][...]
+
+    states = split(node_states[...])
+    list_picks, list_back = picks_of(lists[...], node_rows)
+    outgoing[...] = picked(list_back, states).reshape(4, ghost, width)
+    ghost_copies = halo_copies(outgoing, ghosts, 0)
+    for copy in ghost_copies:
+        copy.start()
+    target_picks, target_back = picks_of(endpoints[1:2, :], node_rows)
+    source_picks, source_back = picks_of(endpoints[0:1, :], node_rows)
+    ghost_picks, ghost_back = picks_of(endpoints[0:1, :], 4 * ghost, node_rows)
+    live_nodes = jnp.where(
+        lax.broadcasted_iota(jnp.int32, (node_rows, 1), 0) < counts[0], 1.0, 0.0
+    ).astype(jnp.float32)
+    live_edges = jnp.where(
+        lax.broadcasted_iota(jnp.int32, (edge_rows, 1), 0) < blocks[0] * 128, 1.0, 0.0
+    ).astype(jnp.float32)
+    edge_act = split(jnp.maximum(edge_pre[...], 0.0))
+    node_act = split(jnp.maximum(node_pre[...], 0.0))
+
+    gather_from_sub(0)
+    gather_from_sub(1)
+    gather_from_x(0)
+    gather_from_sub(2)
+    gather_from_x(1)
+    gather_from_core(0)
+    second_rows = width // (doms * subs)
+    edge_second = split(all_a[:, :, :second_rows, :].reshape(width, width))
+    params = jnp.sum(
+        all_a[:, :, second_rows:, :].reshape(doms * subs, -1, width), axis=0
+    )
+    edge_bias, edge_gain, edge_shift, node_bias, node_gain = (
+        params[row : row + 1, :] for row in range(5)
+    )
+    edge_normed, edge_inverse = layer_norm(wide(edge_act, edge_second, (1, 0)) + edge_bias)
+    message = (edge_normed * edge_gain + edge_shift) * live_edges
+    aggregate = split(picked(target_picks, split(message)))
+
+    gather_from_sub(3)
+    gather_from_x(2)
+    gather_from_core(1)
+    node_second = split(all_b[...].reshape(width, width))
+    node_normed, node_inverse = layer_norm(wide(node_act, node_second, (1, 0)) + node_bias)
+    node_upstream = node_cotangent[...] * live_nodes
+    node_grad_z = split(norm_back(node_upstream * node_gain, node_normed, node_inverse))
+    sum_b[...] = (wide(node_act, node_grad_z, (0, 0)) * node_scale).reshape(sum_b.shape)
+    reduce_core(0)
+    node_grad_pre = split(
+        wide(node_grad_z, node_second, (1, 1)) * (node_pre[...] > 0).astype(jnp.float32)
+    )
+    sum_c[: doms // 2] = (wide(states, node_grad_pre, (0, 0)) * node_scale).reshape(
+        doms // 2, *sum_c.shape[1:]
+    )
+    sum_c[doms // 2 :] = (wide(aggregate, node_grad_pre, (0, 0)) * node_scale).reshape(
+        doms // 2, *sum_c.shape[1:]
+    )
+    reduce_core(1)
+    reduce_core(2)
+
+    gather_from_x(3)
+    gather_from_core(2)
+    for unit in range(3):
+        reduce_x(unit)
+    node_first = split(all_c[...].reshape(2 * width, width))
+    from_nodes = wide(
+        node_grad_pre, tuple(half[width:] for half in node_first), (1, 1)
+    )
+    edge_upstream = (edge_cotangent[...] + picked(target_back, split(from_nodes))) * live_edges
+    edge_grad_z = split(norm_back(edge_upstream * edge_gain, edge_normed, edge_inverse))
+    sum_a[...] = (wide(edge_act, edge_grad_z, (0, 0)) * edge_scale).reshape(sum_a.shape)
+    reduce_core(3)
+    edge_grad_pre = split(
+        wide(edge_grad_z, edge_second, (1, 1)) * (edge_pre[...] > 0).astype(jnp.float32)
+    )
+    for copy in ghost_copies:
+        copy.wait_recv()
+    sender = picked(source_back, states) + picked(
+        ghost_back, split(ghosts[...].reshape(4 * ghost, width))
+    )
+    receiver = picked(target_back, states)
+    first_grad = jnp.concatenate(
+        [
+            wide(split(feature), edge_grad_pre, (0, 0)) * edge_scale
+            for feature in (edge_states[...], sender, receiver)
+        ],
+        axis=0,
+    )
+    sum_d[...] = first_grad.reshape(sum_d.shape)
+    for unit in range(4, len(units)):
+        reduce_core(unit)
+    for unit in range(3):
+        reduce_sub(unit)
+    state_grads = node_upstream + wide(
+        node_grad_pre, tuple(half[:width] for half in node_first), (1, 1)
+    )
+    for unit in range(3, len(units)):
+        reduce_x(unit)
+
+    gather_from_core(3)
+    edge_first = split(all_d[...].reshape(3 * width, width))
+
+    def edge_part(index):
+        rows = slice(index * width, (index + 1) * width)
+        return wide(edge_grad_pre, tuple(half[rows] for half in edge_first), (1, 1))
+
+    sender_grads = split(edge_part(1))
+    ghost_grads[...] = picked(ghost_picks, sender_grads).reshape(4, ghost, width)
+    return_copies = halo_copies(ghost_grads, returned, 1)
+    for copy in return_copies:
+        copy.start()
+    for unit in range(3, 5):
+        reduce_sub(unit)
+    edge_grads[...] = (edge_cotangent[...] + edge_part(0)) * live_edges
+    state_grads = state_grads + picked(source_picks, sender_grads)
+    state_grads = state_grads + picked(target_picks, split(edge_part(2)))
+    for unit in range(5, len(units)):
+        reduce_sub(unit)
+    for copy in return_copies:
+        copy.wait_recv()
+    node_grads[...] = state_grads + picked(
+        list_picks, split(returned[...].reshape(4 * ghost, width))
+    )
+    for unit in range(len(units)):
+        reduce_last(unit)
+
+    for copy in pending + ghost_copies + return_copies:
+        copy.wait_send()
+    for unit in range(len(units)):
+        for copy in core_copies(unit) + [x_copy(unit)] + sub_copies(unit):
+            copy.wait_send()
+
+
+def kernel_shards(
+    node_states,
+    node_pre,
+    edge_states,
+    edge_pre,
+    node_cotangent,
+    edge_cotangent,
+    endpoints,
+    send_lists,
+    node_counts,
+    edge_blocks,
+    edge_first,
+    edge_second,
+    edge_bias,
+    edge_gain,
+    edge_shift,
+    node_first,
+    node_second,
+    node_bias,
+    node_gain,
+):
+    node_rows, width = node_states.shape
+    edge_rows = edge_states.shape[0]
+    ghost = send_lists.shape[2]
+    doms, subs = lax.axis_size("dom"), lax.axis_size("sub")
+    peers = doms * subs
+    mine = lax.axis_index("dom") * subs + lax.axis_index("sub")
+    place = jnp.arange(width) // (width // peers) == mine
+    vectors = jnp.stack([edge_bias, edge_gain, edge_shift, node_bias, node_gain])
+    spread = jnp.where(place[None, :], jnp.tile(vectors, (1, peers)), 0.0)
+    own_a = jnp.concatenate([edge_second, spread, jnp.zeros((3, width), jnp.float32)], axis=0)
+    owns = (own_a, node_second, node_first, edge_first)
+    sums = (node_second, node_first, edge_second, edge_first)
+    units = sum(shard.shape[0] for shard in sums) // UNIT
+    vmem = pl.BlockSpec(memory_space=pltpu.VMEM)
+    smem = pl.BlockSpec(memory_space=pltpu.SMEM)
+    f32 = jnp.float32
+    dma = pltpu.SemaphoreType.DMA
+    halo = pltpu.VMEM((4, ghost, width), f32)
+    return pl.pallas_call(
+        functools.partial(
+            layer_kernel,
+            1.0 / math.sqrt(edge_rows * peers),
+            1.0 / math.sqrt(node_rows * peers),
+        ),
+        out_shape=[
+            jax.ShapeDtypeStruct(shape, f32)
+            for shape in (
+                edge_states.shape,
+                node_states.shape,
+                edge_first.shape,
+                edge_second.shape,
+                node_first.shape,
+                node_second.shape,
+            )
+        ],
+        in_specs=[smem, smem] + [vmem] * 12,
+        out_specs=[vmem] * 6,
+        scratch_shapes=[pltpu.VMEM((doms, subs) + own.shape, f32) for own in owns]
+        + [pltpu.VMEM((doms, subs) + shard.shape, f32) for shard in sums]
+        + [
+            pltpu.VMEM((units, 2, subs, UNIT, width), f32),
+            pltpu.VMEM((units, subs, UNIT, width), f32),
+            pltpu.VMEM((units, subs - 1, UNIT, width), f32),
+            halo,
+            halo,
+            halo,
+            halo,
+            dma((4, 4 * subs - 1)),
+            dma((4, 4 * subs - 1)),
+            dma((units, 2)),
+            dma((units, 2)),
+            dma((units,)),
+            dma((units,)),
+            dma((units, subs - 1)),
+            dma((units, subs - 1)),
+            dma((2, 4)),
+            dma((2, 4)),
+        ],
+        compiler_params=pltpu.CompilerParams(
+            collective_id=0, has_side_effects=True, vmem_limit_bytes=56 * 2**20
+        ),
+    )(
+        node_counts,
+        edge_blocks,
+        endpoints,
+        send_lists.reshape(1, 4 * ghost),
+        node_states,
+        node_pre,
+        edge_states,
+        edge_pre,
+        node_cotangent,
+        edge_cotangent,
+        *owns,
+    )
+
+
+def shards(*blocks):
+    weights = (blocks[10], blocks[11], blocks[15], blocks[16])
+    fits = all(weight.shape[0] % UNIT == 0 for weight in weights)
+    if lax.axis_size("dom") == 4 and lax.axis_size("sub") > 2 and fits:
+        return tuple(kernel_shards(*blocks))
+    return plain_shards(*blocks)
+
+
 def solution(mesh):
     in_specs = (
         P(("groups", "dom", "sub"), None),

time: 443 us -> 123 us (0.28)
  waiting for transfers between devices: 296 us -> 0 us
  Pallas kernels: 0 us -> 111 us
  blocking collectives: 63.6 us -> 0 us
  matrix products: 29 us -> 0 us
  starting transfers between devices: 17.8 us -> 0 us
  between operations: 16.6 us -> 2 us
  other arithmetic: 8.89 us -> 0.73 us
    reduce_scatter x4 -> x0, waiting for transfers between devices: 235 us -> none  [the longest x1 70.1 us: shards(): lax.psum_scatter(inner(features, edge_grad_pre) * edge_scale, ('dom', 'su...]
    pallas_call x0 -> x1, Pallas kernels: none -> 111 us  [kernel_shards(): pl.pallas_call(functools.partial(layer_kernel, 1.0 / math.sqrt(edge_rows...]
    unnamed x1 -> x0, blocking collectives: 63.6 us -> none
    all_gather x4 -> x0, waiting for transfers between devices: 51.9 us -> none  [the longest x1 31.2 us: shards(): lax.all_gather(node_first, ('dom', 'sub'), axis=0, tiled=True)]
    dot_general x10 -> x0, matrix products: 29 us -> none  [the longest x4 12.4 us: outer_back(): lax.dot_general(left, right, (((1,), (1,)), ((), ())), precision=lax.Prec...]
    ppermute x8 -> x0, starting transfers between devices: 17.3 us -> none  [the longest x4 12.2 us: padded(): lax.ppermute(tail, axis, [(i, (i + 1) % count) for i in range(ends)])]
    ppermute x8 -> x0, waiting for transfers between devices: 6.43 us -> none  [the longest x4 4.38 us: padded(): lax.ppermute(head, axis, [((i + 1) % count, i) for i in range(ends)])]
  transfers between devices with their start and end apart: 16 -> 0, of which waited for: 10 -> 0; matrix products, arithmetic and copies ran while one was open for 11% -> 0% of each run, Pallas kernels for 0% -> 0%
where the time goes in v1:
time: 123 us; the launch traced here: 122 us
  Pallas kernels  111 us (90%)
  local copies, waits for them, and re-layouts  8.93 us (7%)
  between operations  2 us (2%)
    pallas_call x1, Pallas kernels, kernel_shards(): pl.pallas_call(functools.partial(layer_kernel, 1.0 / math.sqrt(edge_rows...  111 us
    unnamed x30, local copies, waits for them, and re-layouts  8.16 us

profile of v1, /device:TPU:0, one launch (start us, length us, event | category | flops | bytes accessed | tf_op | source)
XLA Modules:
  0.0 122.3 jit_solution(327283448268608404)
XLA Ops:
  1.9 0.0 copy-start.6
  2.0 0.7 copy-done.6
  2.6 0.6 reshape.33.lists
  3.2 0.0 copy-start.10
  3.2 0.0 copy-start.11
  3.2 0.0 copy-start.7
  3.2 0.0 copy-start.8
  3.2 0.0 copy-start.9
  3.3 0.1 pad.2.clone
  3.3 0.5 copy-done.10
  3.9 0.0 copy-done.11
  3.9 0.0 copy-done.7
  3.9 0.0 copy-done.8
  3.9 0.0 copy-done.9
  4.0 0.0 copy-start.3
  4.0 0.1 tile.10
  4.1 0.7 copy-done.3
  4.8 0.7 maximum_maximum_fusion.own_a
  5.5 110.6 %shard_map.226 = (f32[128,512]{1,0:T(8,128)}, f32[256,512]{1,0:T(8,128)}, f32[96,512]{1,0:T(8,128)}, f32[32,512]{1,0:T(8,128)}, f32[64,512]{1,0:T(8,128)}, /*index=5*/f32[32,512]{1,0:T(8,128)}) custom-call(s32[1]{0:T(128)S(6)} %copy.31.counts, s32[1]{0:T(128)S(6)} %copy.32.blocks, s32[2,128]{1,0:T(2,128)} %endpoints.1, s32[1,64]{1,0:T(1,128)} %reshape.33.lists, ...), custom_call_target="tpu_custom_call" | custom-call | tf_op jit(solution)/shard_map/pallas_call | solution.py:631
  116.1 0.0 copy-start
  116.1 1.7 %copy.33 = f32[128,512]{1,0:T(8,128)} copy(f32[128,512]{1,0:T(8,128)} %get-tuple-element.12) | data formatting | bytes 524288
  117.8 0.0 copy-done
  117.8 0.0 copy-start.1
  117.9 0.8 copy.34
  118.6 0.3 copy-done.1
  119.0 0.0 copy-start.5
  119.0 0.7 copy.35
  119.6 0.2 copy-done.5
  119.8 0.0 copy-start.2
  119.8 0.6 copy.36
  120.5 0.3 copy-done.2
  120.8 0.0 copy-start.4
  120.8 0.7 copy.37
  121.4 0.2 copy-done.4
  121.6 0.6 copy.38
  (5 shorter events, 0.0 us)
Async XLA Ops:
  1.9 0.7 copy-start.6
  3.2 0.7 copy-start.10
  3.2 0.7 copy-start.11
  3.2 0.7 copy-start.7
  3.2 0.7 copy-start.8
  3.2 0.7 copy-start.9
  4.0 0.8 copy-start.3
  116.1 1.7 %copy-start = (f32[256,512]{1,0:T(8,128)S(1)}, f32[256,512]{1,0:T(8,128)}, u32[]{:S(2)}) copy-start(f32[256,512]{1,0:T(8,128)} %get-tuple-element.13) | copy-start | bytes 1572868
  117.8 1.1 copy-start.1
  119.0 0.9 copy-start.5
  119.8 0.9 copy-start.2
  120.8 0.9 copy-start.4

commit v2 on v1

--- a/solution.py
+++ b/solution.py
@@ -274,6 +274,7 @@
     ghost = outgoing.shape[1]
     dom = lax.axis_index("dom")
     sub = lax.axis_index("sub")
+    group = lax.axis_index("groups")
     x_mate = lax.rem(dom + 2, doms)
     core_mate = dom + 1 - 2 * lax.rem(dom, 2)
     far_mate = x_mate + 1 - 2 * lax.rem(x_mate, 2)
@@ -291,7 +292,8 @@
         )
     for step in range(1, subs):
         pl.semaphore_signal(barrier, inc=1, device_id={"sub": after(step)}, device_id_type=MESH)
-    pl.semaphore_wait(barrier, doms + subs - 2)
+    pl.semaphore_signal(barrier, inc=1, device_id={"groups": 1 - group}, device_id_type=MESH)
+    pl.semaphore_wait(barrier, doms + subs - 1)
 
     def remote(source, target, send, recv, device):
         return pltpu.make_async_remote_copy(
@@ -305,61 +307,82 @@
 
     owns = (own_a, own_b, own_c, own_d)
     alls = (all_a, all_b, all_c, all_d)
+    shared = (False, False, True, True)
     pending = []
 
-    def gather_copy(part, index, source, slot, device):
+    def rows_of(ref, part, half):
+        if half is None or not shared[part]:
+            return ref
+        count = owns[part].shape[0] // 2
+        return ref.at[pl.ds(pl.multiple_of(half * count, 16), count), :]
+
+    def place_of(part, slot, half):
+        return rows_of(alls[part].at[slot[0], slot[1]], part, half)
+
+    def gather_copy(part, index, source, target, device):
         return remote(
-            source,
-            alls[part].at[slot[0], slot[1]],
-            gather_send.at[part, index],
-            gather_recv.at[part, index],
-            device,
+            source, target, gather_send.at[part, index], gather_recv.at[part, index], device
         )
 
-    def gather_start(part, index, source, slot, device):
-        copy = gather_copy(part, index, source, slot, device)
+    def gather_start(part, index, slot, half, device, own=False):
+        target = place_of(part, slot, half)
+        source = rows_of(owns[part], part, half) if own else target
+        copy = gather_copy(part, index, source, target, device)
         copy.start()
         pending.append(copy)
 
-    def gather_wait(part, index, slot):
-        place = alls[part].at[slot[0], slot[1]]
-        gather_copy(part, index, place, slot, {"dom": core_mate}).wait_recv()
-
-    def to_x(part, step, source):
-        gather_start(part, subs - 1 + step, source, (dom, before(step)), {"dom": x_mate})
-
-    def to_core(part, step, source):
-        gather_start(part, 2 * subs - 1 + step, source, (dom, before(step)), {"dom": core_mate})
+    def gather_wait(part, index, slot, half):
+        place = place_of(part, slot, half)
+        gather_copy(part, index, place, place, {"dom": core_mate}).wait_recv()
+
+    SUB, X = 0, subs - 1
+    CORE_NEAR, CORE_FAR = 2 * subs - 1, 3 * subs - 1
+    Y_NEAR, Y_FAR = 4 * subs - 1, 5 * subs - 1
+    LATE_NEAR, LATE_FAR = 6 * subs - 1, 7 * subs - 1
+    to_x, to_core, to_y = {"dom": x_mate}, {"dom": core_mate}, {"groups": 1 - group}
 
     def gather_first(part):
         for step in range(1, subs):
-            gather_start(part, step - 1, owns[part], (dom, sub), {"sub": after(step)})
-        to_x(part, 0, owns[part])
-        to_core(part, 0, owns[part])
-
-    def gather_from_sub(part):
-        for step in range(1, subs):
+            gather_start(part, SUB + step - 1, (dom, sub), group, {"sub": after(step)}, True)
+        gather_start(part, X, (dom, sub), group, to_x, True)
+        gather_start(part, CORE_NEAR, (dom, sub), None, to_core, True)
+
+    def gather_from_sub(part, steps=range(1, subs)):
+        for step in steps:
             slot = (dom, before(step))
-            gather_wait(part, step - 1, slot)
-            to_x(part, step, alls[part].at[slot[0], slot[1]])
-            to_core(part, step, alls[part].at[slot[0], slot[1]])
+            gather_wait(part, SUB + step - 1, slot, group)
+            gather_start(part, X + step, slot, group, to_x)
+            if shared[part]:
+                gather_start(part, Y_NEAR + step, slot, group, to_y)
+            gather_start(part, CORE_NEAR + step, slot, group, to_core)
 
     def gather_from_x(part):
         for step in range(subs):
             slot = (x_mate, before(step))
-            gather_wait(part, subs - 1 + step, slot)
-            gather_start(
-                part,
-                3 * subs - 1 + step,
-                alls[part].at[slot[0], slot[1]],
-                slot,
-                {"dom": core_mate},
-            )
+            gather_wait(part, X + step, slot, group)
+            if shared[part]:
+                gather_start(part, Y_FAR + step, slot, group, to_y)
+            gather_start(part, CORE_FAR + step, slot, group, to_core)
+
+    def gather_from_y(part):
+        for step in range(1, subs):
+            slot = (dom, before(step))
+            gather_wait(part, Y_NEAR + step, slot, 1 - group)
+            gather_start(part, LATE_NEAR + step, slot, 1 - group, to_core)
+        for step in range(subs):
+            slot = (x_mate, before(step))
+            gather_wait(part, Y_FAR + step, slot, 1 - group)
+            gather_start(part, LATE_FAR + step, slot, 1 - group, to_core)
 
     def gather_from_core(part):
         for step in range(subs):
-            gather_wait(part, 2 * subs - 1 + step, (core_mate, before(step)))
-            gather_wait(part, 3 * subs - 1 + step, (far_mate, before(step)))
+            near, far = (core_mate, before(step)), (far_mate, before(step))
+            gather_wait(part, CORE_NEAR + step, near, group if step else None)
+            gather_wait(part, CORE_FAR + step, far, group)
+            if shared[part]:
+                if step:
+                    gather_wait(part, LATE_NEAR + step, near, 1 - group)
+                gather_wait(part, LATE_FAR + step, far, 1 - group)
 
     sums = (sum_b, sum_c, sum_a, sum_d)
     results = (node_second_grad, node_first_grad, edge_second_grad, edge_first_grad)
@@ -454,7 +477,7 @@
             for index in range(4)
         ]
 
-    for part in range(4):
+    for part in range(2):
         gather_first(part)
     for part in range(4):
         alls[part][dom, sub] = owns[part][...]
@@ -478,9 +501,9 @@
     node_act = split(jnp.maximum(node_pre[...], 0.0))
 
     gather_from_sub(0)
+    gather_first(2)
     gather_from_sub(1)
     gather_from_x(0)
-    gather_from_sub(2)
     gather_from_x(1)
     gather_from_core(0)
     second_rows = width // (doms * subs)
@@ -495,18 +518,21 @@
     message = (edge_normed * edge_gain + edge_shift) * live_edges
     aggregate = split(picked(target_picks, split(message)))
 
-    gather_from_sub(3)
-    gather_from_x(2)
+    gather_from_sub(2, [1])
     gather_from_core(1)
     node_second = split(all_b[...].reshape(width, width))
     node_normed, node_inverse = layer_norm(wide(node_act, node_second, (1, 0)) + node_bias)
+    gather_from_sub(2, range(2, subs))
+    gather_first(3)
     node_upstream = node_cotangent[...] * live_nodes
     node_grad_z = split(norm_back(node_upstream * node_gain, node_normed, node_inverse))
+    gather_from_x(2)
     sum_b[...] = (wide(node_act, node_grad_z, (0, 0)) * node_scale).reshape(sum_b.shape)
     reduce_core(0)
     node_grad_pre = split(
         wide(node_grad_z, node_second, (1, 1)) * (node_pre[...] > 0).astype(jnp.float32)
     )
+    gather_from_y(2)
     sum_c[: doms // 2] = (wide(states, node_grad_pre, (0, 0)) * node_scale).reshape(
         doms // 2, *sum_c.shape[1:]
     )
@@ -516,21 +542,25 @@
     reduce_core(1)
     reduce_core(2)
 
-    gather_from_x(3)
+    gather_from_sub(3, range(1, subs - 1))
+    reduce_x(0)
     gather_from_core(2)
-    for unit in range(3):
-        reduce_x(unit)
+    reduce_x(1)
+    reduce_x(2)
     node_first = split(all_c[...].reshape(2 * width, width))
     from_nodes = wide(
         node_grad_pre, tuple(half[width:] for half in node_first), (1, 1)
     )
     edge_upstream = (edge_cotangent[...] + picked(target_back, split(from_nodes))) * live_edges
     edge_grad_z = split(norm_back(edge_upstream * edge_gain, edge_normed, edge_inverse))
+    gather_from_sub(3, [subs - 1])
     sum_a[...] = (wide(edge_act, edge_grad_z, (0, 0)) * edge_scale).reshape(sum_a.shape)
     reduce_core(3)
     edge_grad_pre = split(
         wide(edge_grad_z, edge_second, (1, 1)) * (edge_pre[...] > 0).astype(jnp.float32)
     )
+    gather_from_x(3)
+    reduce_sub(0)
     for copy in ghost_copies:
         copy.wait_recv()
     sender = picked(source_back, states) + picked(
@@ -547,13 +577,15 @@
     sum_d[...] = first_grad.reshape(sum_d.shape)
     for unit in range(4, len(units)):
         reduce_core(unit)
-    for unit in range(3):
-        reduce_sub(unit)
+    reduce_x(3)
+    reduce_sub(1)
+    reduce_sub(2)
+    gather_from_y(3)
+    for unit in range(4, len(units)):
+        reduce_x(unit)
     state_grads = node_upstream + wide(
         node_grad_pre, tuple(half[:width] for half in node_first), (1, 1)
     )
-    for unit in range(3, len(units)):
-        reduce_x(unit)
 
     gather_from_core(3)
     edge_first = split(all_d[...].reshape(3 * width, width))
@@ -657,8 +689,8 @@
             halo,
             halo,
             halo,
-            dma((4, 4 * subs - 1)),
-            dma((4, 4 * subs - 1)),
+            dma((4, 8 * subs - 1)),
+            dma((4, 8 * subs - 1)),
             dma((units, 2)),
             dma((units, 2)),
             dma((units,)),
@@ -689,7 +721,8 @@
 def shards(*blocks):
     weights = (blocks[10], blocks[11], blocks[15], blocks[16])
     fits = all(weight.shape[0] % UNIT == 0 for weight in weights)
-    if lax.axis_size("dom") == 4 and lax.axis_size("sub") > 2 and fits:
+    paired = lax.axis_size("groups") == 2 and lax.axis_size("dom") == 4
+    if paired and lax.axis_size("sub") > 2 and fits:
         return tuple(kernel_shards(*blocks))
     return plain_shards(*blocks)
 

time: 123 us -> 124 us (level)
  no operation moved by 1% of the time
where the time goes in v2:
time: 124 us; the launch traced here: 123 us
  Pallas kernels  112 us (90%)
  local copies, waits for them, and re-layouts  8.93 us (7%)
  between operations  2 us (2%)
    pallas_call x1, Pallas kernels, kernel_shards(): pl.pallas_call(functools.partial(layer_kernel, 1.0 / math.sqrt(edge_rows...  112 us
    unnamed x30, local copies, waits for them, and re-layouts  8.16 us

profile of v2, /device:TPU:0, one launch (start us, length us, event | category | flops | bytes accessed | tf_op | source)
XLA Modules:
  0.0 123.2 jit_solution(18337227673376910823)
XLA Ops:
  1.9 0.0 copy-start.6
  2.0 0.7 copy-done.6
  2.6 0.6 reshape.33.lists
  3.2 0.0 copy-start.10
  3.2 0.0 copy-start.11
  3.2 0.0 copy-start.7
  3.2 0.0 copy-start.8
  3.2 0.0 copy-start.9
  3.3 0.1 pad.2.clone
  3.3 0.5 copy-done.10
  3.9 0.0 copy-done.11
  3.9 0.0 copy-done.7
  3.9 0.0 copy-done.8
  3.9 0.0 copy-done.9
  4.0 0.0 copy-start.3
  4.0 0.1 tile.10
  4.1 0.7 copy-done.3
  4.8 0.7 maximum_maximum_fusion.own_a
  5.5 111.5 %shard_map.226 = (f32[128,512]{1,0:T(8,128)}, f32[256,512]{1,0:T(8,128)}, f32[96,512]{1,0:T(8,128)}, f32[32,512]{1,0:T(8,128)}, f32[64,512]{1,0:T(8,128)}, /*index=5*/f32[32,512]{1,0:T(8,128)}) custom-call(s32[1]{0:T(128)S(6)} %copy.31.counts, s32[1]{0:T(128)S(6)} %copy.32.blocks, s32[2,128]{1,0:T(2,128)} %endpoints.1, s32[1,64]{1,0:T(1,128)} %reshape.33.lists, ...), custom_call_target="tpu_custom_call" | custom-call | tf_op jit(solution)/shard_map/pallas_call | solution.py:663
  117.0 0.0 copy-start
  117.0 1.7 %copy.33 = f32[128,512]{1,0:T(8,128)} copy(f32[128,512]{1,0:T(8,128)} %get-tuple-element.12) | data formatting | bytes 524288
  118.8 0.0 copy-done
  118.8 0.0 copy-start.1
  118.8 0.8 copy.34
  119.6 0.3 copy-done.1
  119.9 0.0 copy-start.5
  119.9 0.7 copy.35
  120.6 0.2 copy-done.5
  120.8 0.0 copy-start.2
  120.8 0.6 copy.36
  121.4 0.3 copy-done.2
  121.7 0.0 copy-start.4
  121.7 0.7 copy.37
  122.3 0.2 copy-done.4
  122.6 0.6 copy.38
  (5 shorter events, 0.0 us)
Async XLA Ops:
  1.9 0.7 copy-start.6
  3.2 0.7 copy-start.10
  3.2 0.7 copy-start.11
  3.2 0.7 copy-start.7
  3.2 0.7 copy-start.8
  3.2 0.7 copy-start.9
  4.0 0.8 copy-start.3
  117.0 1.7 %copy-start = (f32[256,512]{1,0:T(8,128)S(1)}, f32[256,512]{1,0:T(8,128)}, u32[]{:S(2)}) copy-start(f32[256,512]{1,0:T(8,128)} %get-tuple-element.13) | copy-start | bytes 1572868
  118.8 1.1 copy-start.1
  119.9 0.9 copy-start.5
  120.8 0.9 copy-start.2
  121.7 0.9 copy-start.4

commit v3 on v2

--- a/solution.py
+++ b/solution.py
@@ -503,70 +503,71 @@
     gather_from_sub(0)
     gather_first(2)
     gather_from_sub(1)
+    gather_first(3)
     gather_from_x(0)
-    gather_from_x(1)
     gather_from_core(0)
     second_rows = width // (doms * subs)
-    edge_second = split(all_a[:, :, :second_rows, :].reshape(width, width))
+    node_second = split(all_a[:, :, :second_rows, :].reshape(width, width))
     params = jnp.sum(
         all_a[:, :, second_rows:, :].reshape(doms * subs, -1, width), axis=0
     )
     edge_bias, edge_gain, edge_shift, node_bias, node_gain = (
         params[row : row + 1, :] for row in range(5)
     )
+    node_normed, node_inverse = layer_norm(wide(node_act, node_second, (1, 0)) + node_bias)
+    gather_from_x(1)
+    gather_from_sub(2, [1])
+    node_upstream = node_cotangent[...] * live_nodes
+    node_grad_z = split(norm_back(node_upstream * node_gain, node_normed, node_inverse))
+    gather_from_sub(2, range(2, subs))
+    sum_b[...] = (wide(node_act, node_grad_z, (0, 0)) * node_scale).reshape(sum_b.shape)
+    reduce_core(0)
+    gather_from_core(1)
+    edge_second = split(all_b[...].reshape(width, width))
     edge_normed, edge_inverse = layer_norm(wide(edge_act, edge_second, (1, 0)) + edge_bias)
     message = (edge_normed * edge_gain + edge_shift) * live_edges
     aggregate = split(picked(target_picks, split(message)))
-
-    gather_from_sub(2, [1])
-    gather_from_core(1)
-    node_second = split(all_b[...].reshape(width, width))
-    node_normed, node_inverse = layer_norm(wide(node_act, node_second, (1, 0)) + node_bias)
-    gather_from_sub(2, range(2, subs))
-    gather_first(3)
-    node_upstream = node_cotangent[...] * live_nodes
-    node_grad_z = split(norm_back(node_upstream * node_gain, node_normed, node_inverse))
     gather_from_x(2)
-    sum_b[...] = (wide(node_act, node_grad_z, (0, 0)) * node_scale).reshape(sum_b.shape)
-    reduce_core(0)
+    gather_from_sub(3, [1])
+    reduce_x(0)
     node_grad_pre = split(
         wide(node_grad_z, node_second, (1, 1)) * (node_pre[...] > 0).astype(jnp.float32)
     )
-    gather_from_y(2)
+    gather_from_sub(3, range(2, subs))
     sum_c[: doms // 2] = (wide(states, node_grad_pre, (0, 0)) * node_scale).reshape(
         doms // 2, *sum_c.shape[1:]
     )
+    gather_from_y(2)
     sum_c[doms // 2 :] = (wide(aggregate, node_grad_pre, (0, 0)) * node_scale).reshape(
         doms // 2, *sum_c.shape[1:]
     )
     reduce_core(1)
     reduce_core(2)
-
-    gather_from_sub(3, range(1, subs - 1))
-    reduce_x(0)
+    gather_from_x(3)
     gather_from_core(2)
     reduce_x(1)
     reduce_x(2)
+
     node_first = split(all_c[...].reshape(2 * width, width))
     from_nodes = wide(
         node_grad_pre, tuple(half[width:] for half in node_first), (1, 1)
     )
     edge_upstream = (edge_cotangent[...] + picked(target_back, split(from_nodes))) * live_edges
     edge_grad_z = split(norm_back(edge_upstream * edge_gain, edge_normed, edge_inverse))
-    gather_from_sub(3, [subs - 1])
     sum_a[...] = (wide(edge_act, edge_grad_z, (0, 0)) * edge_scale).reshape(sum_a.shape)
     reduce_core(3)
+    reduce_sub(0)
+    gather_from_y(3)
     edge_grad_pre = split(
         wide(edge_grad_z, edge_second, (1, 1)) * (edge_pre[...] > 0).astype(jnp.float32)
     )
-    gather_from_x(3)
-    reduce_sub(0)
     for copy in ghost_copies:
         copy.wait_recv()
     sender = picked(source_back, states) + picked(
         ghost_back, split(ghosts[...].reshape(4 * ghost, width))
     )
     receiver = picked(target_back, states)
+    reduce_x(3)
     first_grad = jnp.concatenate(
         [
             wide(split(feature), edge_grad_pre, (0, 0)) * edge_scale
@@ -577,12 +578,10 @@
     sum_d[...] = first_grad.reshape(sum_d.shape)
     for unit in range(4, len(units)):
         reduce_core(unit)
-    reduce_x(3)
     reduce_sub(1)
-    reduce_sub(2)
-    gather_from_y(3)
     for unit in range(4, len(units)):
         reduce_x(unit)
+    reduce_sub(2)
     state_grads = node_upstream + wide(
         node_grad_pre, tuple(half[:width] for half in node_first), (1, 1)
     )
@@ -651,8 +650,8 @@
     place = jnp.arange(width) // (width // peers) == mine
     vectors = jnp.stack([edge_bias, edge_gain, edge_shift, node_bias, node_gain])
     spread = jnp.where(place[None, :], jnp.tile(vectors, (1, peers)), 0.0)
-    own_a = jnp.concatenate([edge_second, spread, jnp.zeros((3, width), jnp.float32)], axis=0)
-    owns = (own_a, node_second, node_first, edge_first)
+    own_a = jnp.concatenate([node_second, spread, jnp.zeros((3, width), jnp.float32)], axis=0)
+    owns = (own_a, edge_second, node_first, edge_first)
     sums = (node_second, node_first, edge_second, edge_first)
     units = sum(shard.shape[0] for shard in sums) // UNIT
     vmem = pl.BlockSpec(memory_space=pltpu.VMEM)

time: 124 us -> 109 us (0.88)
  Pallas kernels: 112 us -> 97.4 us
    pallas_call x1, Pallas kernels: 112 us -> 97.4 us  [kernel_shards(): pl.pallas_call(functools.partial(layer_kernel, 1.0 / math.sqrt(edge_rows...]
where the time goes in v3:
time: 109 us
  Pallas kernels  97.4 us (89%)
  local copies, waits for them, and re-layouts  8.93 us (8%)
  between operations  2 us (2%)
    pallas_call x1, Pallas kernels, kernel_shards(): pl.pallas_call(functools.partial(layer_kernel, 1.0 / math.sqrt(edge_rows...  97.4 us
    unnamed x30, local copies, waits for them, and re-layouts  8.16 us

profile of v3, /device:TPU:0, one launch (start us, length us, event | category | flops | bytes accessed | tf_op | source)
XLA Modules:
  0.0 109.1 jit_solution(9100895871759438593)
XLA Ops:
  1.9 0.0 copy-start.6
  2.0 0.7 copy-done.6
  2.6 0.6 reshape.33.lists
  3.2 0.0 copy-start.10
  3.2 0.0 copy-start.11
  3.2 0.0 copy-start.7
  3.2 0.0 copy-start.8
  3.2 0.0 copy-start.9
  3.3 0.1 pad.2.clone
  3.3 0.5 copy-done.10
  3.9 0.0 copy-done.11
  3.9 0.0 copy-done.7
  3.9 0.0 copy-done.8
  3.9 0.0 copy-done.9
  4.0 0.0 copy-start.3
  4.0 0.1 tile.10
  4.1 0.7 copy-done.3
  4.8 0.7 maximum_maximum_fusion.own_a
  5.5 97.4 %shard_map.226 = (f32[128,512]{1,0:T(8,128)}, f32[256,512]{1,0:T(8,128)}, f32[96,512]{1,0:T(8,128)}, f32[32,512]{1,0:T(8,128)}, f32[64,512]{1,0:T(8,128)}, /*index=5*/f32[32,512]{1,0:T(8,128)}) custom-call(s32[1]{0:T(128)S(6)} %copy.31.counts, s32[1]{0:T(128)S(6)} %copy.32.blocks, s32[2,128]{1,0:T(2,128)} %endpoints.1, s32[1,64]{1,0:T(1,128)} %reshape.33.lists, ...), custom_call_target="tpu_custom_call" | custom-call | tf_op jit(solution)/shard_map/pallas_call | solution.py:662
  102.9 0.0 copy-start
  102.9 1.7 %copy.33 = f32[128,512]{1,0:T(8,128)} copy(f32[128,512]{1,0:T(8,128)} %get-tuple-element.12) | data formatting | bytes 524288
  104.7 0.0 copy-done
  104.7 0.0 copy-start.1
  104.7 0.8 copy.34
  105.5 0.3 copy-done.1
  105.8 0.0 copy-start.5
  105.8 0.7 copy.35
  106.5 0.2 copy-done.5
  106.6 0.0 copy-start.2
  106.6 0.6 copy.36
  107.3 0.3 copy-done.2
  107.6 0.0 copy-start.4
  107.6 0.7 copy.37
  108.2 0.2 copy-done.4
  108.4 0.6 copy.38
  (5 shorter events, 0.0 us)
Async XLA Ops:
  1.9 0.7 copy-start.6
  3.2 0.7 copy-start.10
  3.2 0.7 copy-start.11
  3.2 0.7 copy-start.7
  3.2 0.7 copy-start.8
  3.2 0.7 copy-start.9
  4.0 0.8 copy-start.3
  102.9 1.7 %copy-start = (f32[256,512]{1,0:T(8,128)S(1)}, f32[256,512]{1,0:T(8,128)}, u32[]{:S(2)}) copy-start(f32[256,512]{1,0:T(8,128)} %get-tuple-element.13) | copy-start | bytes 1572868
  104.7 1.1 %copy-start.1 = (f32[96,512]{1,0:T(8,128)S(1)}, f32[96,512]{1,0:T(8,128)}, u32[]{:S(2)}) copy-start(f32[96,512]{1,0:T(8,128)} %get-tuple-element.14) | copy-start | bytes 589828
  105.8 0.9 copy-start.5
  106.6 0.9 copy-start.2
  107.6 0.9 copy-start.4

commit v4 on v3

--- a/solution.py
+++ b/solution.py
@@ -568,6 +568,8 @@
     )
     receiver = picked(target_back, states)
     reduce_x(3)
+    reduce_sub(1)
+    reduce_sub(2)
     first_grad = jnp.concatenate(
         [
             wide(split(feature), edge_grad_pre, (0, 0)) * edge_scale
@@ -578,10 +580,9 @@
     sum_d[...] = first_grad.reshape(sum_d.shape)
     for unit in range(4, len(units)):
         reduce_core(unit)
-    reduce_sub(1)
     for unit in range(4, len(units)):
         reduce_x(unit)
-    reduce_sub(2)
+    reduce_sub(3)
     state_grads = node_upstream + wide(
         node_grad_pre, tuple(half[:width] for half in node_first), (1, 1)
     )
@@ -598,8 +599,7 @@
     return_copies = halo_copies(ghost_grads, returned, 1)
     for copy in return_copies:
         copy.start()
-    for unit in range(3, 5):
-        reduce_sub(unit)
+    reduce_sub(4)
     edge_grads[...] = (edge_cotangent[...] + edge_part(0)) * live_edges
     state_grads = state_grads + picked(source_picks, sender_grads)
     state_grads = state_grads + picked(target_picks, split(edge_part(2)))

time: 109 us -> 108 us (level); the launches traced: 109 us -> 107 us
  Pallas kernels: 97.4 us -> 95.1 us
    pallas_call x1, Pallas kernels: 97.4 us -> 95.1 us  [kernel_shards(): pl.pallas_call(functools.partial(layer_kernel, 1.0 / math.sqrt(edge_rows...]
where the time goes in v4:
time: 108 us; the launch traced here: 107 us
  Pallas kernels  95.1 us (88%)
  local copies, waits for them, and re-layouts  8.93 us (8%)
  between operations  2 us (2%)
    pallas_call x1, Pallas kernels, kernel_shards(): pl.pallas_call(functools.partial(layer_kernel, 1.0 / math.sqrt(edge_rows...  95.1 us
    unnamed x30, local copies, waits for them, and re-layouts  8.16 us

profile of v4, /device:TPU:0, one launch (start us, length us, event | category | flops | bytes accessed | tf_op | source)
XLA Modules:
  0.0 106.7 jit_solution(13592315157376611706)
XLA Ops:
  1.9 0.0 copy-start.6
  2.0 0.7 copy-done.6
  2.6 0.6 reshape.33.lists
  3.2 0.0 copy-start.10
  3.2 0.0 copy-start.11
  3.2 0.0 copy-start.7
  3.2 0.0 copy-start.8
  3.2 0.0 copy-start.9
  3.3 0.1 pad.2.clone
  3.3 0.5 copy-done.10
  3.9 0.0 copy-done.11
  3.9 0.0 copy-done.7
  3.9 0.0 copy-done.8
  3.9 0.0 copy-done.9
  4.0 0.0 copy-start.3
  4.0 0.1 tile.10
  4.1 0.7 copy-done.3
  4.8 0.7 maximum_maximum_fusion.own_a
  5.5 95.1 %shard_map.226 = (f32[128,512]{1,0:T(8,128)}, f32[256,512]{1,0:T(8,128)}, f32[96,512]{1,0:T(8,128)}, f32[32,512]{1,0:T(8,128)}, f32[64,512]{1,0:T(8,128)}, /*index=5*/f32[32,512]{1,0:T(8,128)}) custom-call(s32[1]{0:T(128)S(6)} %copy.31.counts, s32[1]{0:T(128)S(6)} %copy.32.blocks, s32[2,128]{1,0:T(2,128)} %endpoints.1, s32[1,64]{1,0:T(1,128)} %reshape.33.lists, ...), custom_call_target="tpu_custom_call" | custom-call | tf_op jit(solution)/shard_map/pallas_call | solution.py:662
  100.6 0.0 copy-start
  100.6 1.7 %copy.33 = f32[128,512]{1,0:T(8,128)} copy(f32[128,512]{1,0:T(8,128)} %get-tuple-element.12) | data formatting | bytes 524288
  102.3 0.0 copy-done
  102.3 0.0 copy-start.1
  102.3 0.8 copy.34
  103.1 0.3 copy-done.1
  103.5 0.0 copy-start.5
  103.5 0.7 copy.35
  104.1 0.2 copy-done.5
  104.3 0.0 copy-start.2
  104.3 0.6 copy.36
  105.0 0.3 copy-done.2
  105.2 0.0 copy-start.4
  105.3 0.7 copy.37
  105.9 0.2 copy-done.4
  106.1 0.6 copy.38
  (5 shorter events, 0.0 us)
Async XLA Ops:
  1.9 0.7 copy-start.6
  3.2 0.7 copy-start.10
  3.2 0.7 copy-start.11
  3.2 0.7 copy-start.7
  3.2 0.7 copy-start.8
  3.2 0.7 copy-start.9
  4.0 0.8 copy-start.3
  100.6 1.7 %copy-start = (f32[256,512]{1,0:T(8,128)S(1)}, f32[256,512]{1,0:T(8,128)}, u32[]{:S(2)}) copy-start(f32[256,512]{1,0:T(8,128)} %get-tuple-element.13) | copy-start | bytes 1572868
  102.3 1.1 %copy-start.1 = (f32[96,512]{1,0:T(8,128)S(1)}, f32[96,512]{1,0:T(8,128)}, u32[]{:S(2)}) copy-start(f32[96,512]{1,0:T(8,128)} %get-tuple-element.14) | copy-start | bytes 589828
  103.5 0.9 copy-start.5
  104.3 0.9 copy-start.2
  105.2 0.9 copy-start.4
